TPU v7x, 128 devices: a whole 4x4x4 slice. The times are simulated.
128 devices in a mesh: blk: 32 (over z, y_hi, x), rep: 4 (over y_lo, core).
Axes of the slice: x: 4, y: 4 (y_hi: 2, y_lo: 2; y = y_hi * 2 + y_lo), z: 4, core: 2. Of those that a mesh axis runs over, the one named last changes fastest.
Arguments:
- features: bfloat16 [16384, 128], P(('blk', 'rep'))
- owner_row: int32 [16384], P(('blk', 'rep')), may hold values from 0 to 16383, as said below
- value_probe: bfloat16 [8, 16384], P(None, 'blk'), may hold values from -6 to 6
- grad_probe: bfloat16 [16384, 1024], P('blk'), may hold values from -6 to 6
Outputs:
- value_out: float32 [8, 16384], P(None, ('blk', 'rep'))
- grad_out: float32 [16384, 1024], P(('blk', 'rep'))
Inputs may be any that keep to these rules, and one draw needn't show every extreme that they name: `owner_row`: A permutation. The data shard of device (a, r), rows (a 4 + r) * 128 to (a 4 + r + 1) * 128 - 1 with blk index a and rep index r, sends exactly 4 rows to every row block b, all into that block's rows b * 512 + r * 128 to b * 512 + (r + 1) * 128 - 1.
All inputs are finite; a program needn't handle non-finite values.
Results may differ from a plain program's by a relative error of at most 0.002.
Values may be sent and summed in bfloat16 or wider, within the bound.
A program may use at most 64 MiB of HBM per device.

v0:
```python
import jax
import jax.numpy as jnp
from jax import lax
from jax.sharding import PartitionSpec as P


def shortened(array):
    return jax.tree.map(lambda a: a.astype(jnp.bfloat16) if a.dtype == jnp.float32 else a, array)


def passed_along(block, axis, distance):
    devices = range(lax.axis_size(axis))
    route = [((i - distance) % len(devices), i) for i in devices]
    return lax.ppermute(block, axis, route)


def pair_terms(own_rows, column, scaling, totals):
    col_rows, col_values, col_grads = column
    values, grads = totals
    square = scaling * scaling
    row_count, width = own_rows.shape
    probes = col_values.shape[0]
    own_wide = own_rows.astype(jnp.float32)
    col_wide = col_rows.astype(jnp.float32)
    own_norm = jnp.sum(own_wide * own_wide, 1)
    col_norm = jnp.sum(col_wide * col_wide, 1)
    gram = jnp.einsum("id,jd->ij", own_rows, col_rows, preferred_element_type=jnp.float32)
    kernel = jnp.exp(
        -0.5 * (square * own_norm[:, None] + square * col_norm[None, :] - 2.0 * square * gram)
    )
    shaped = col_grads.reshape(col_rows.shape[0], probes, width)
    anchor = (
        jnp.einsum("jd,jpd->pj", col_rows, shaped, preferred_element_type=jnp.float32) * scaling
    )
    inner = (
        jnp.einsum("id,jpd->ipj", own_rows, shaped, preferred_element_type=jnp.float32) * scaling
        - anchor[None]
    )
    coef = kernel[:, None, :] * (col_values.astype(jnp.float32)[None] + inner)
    sums = jnp.sum(coef, 2)
    coef_low = coef.astype(jnp.bfloat16).reshape(row_count * probes, col_rows.shape[0])
    cross = (
        jnp.dot(coef_low, col_rows, preferred_element_type=jnp.float32).reshape(
            row_count, probes * width
        )
        * scaling
    )
    spread = jnp.dot(kernel.astype(jnp.bfloat16), col_grads, preferred_element_type=jnp.float32)
    pull = ((own_wide * scaling)[:, None, :] * sums[:, :, None]).reshape(row_count, probes * width)
    return (values + sums, grads + spread + cross - pull)


def per_device(features, owner_row, value_probe, grad_probe):
    quarter = features.shape[0]
    width = features.shape[1]
    block_count = lax.axis_size("blk")
    copies = lax.axis_size("rep")
    block_rows = quarter * copies
    group_rows = quarter // block_count
    probes = value_probe.shape[0]
    scaling = (4.0 * width) ** (-0.25)
    order = jnp.argsort(owner_row)
    outgoing = features[order].reshape(block_count, group_rows, width)
    slots = (owner_row % quarter)[order].reshape(block_count, group_rows)
    arrived, arrived_slots = (
        lax.all_to_all(outgoing, "blk", split_axis=0, concat_axis=0, tiled=True),
        lax.all_to_all(slots, "blk", split_axis=0, concat_axis=0, tiled=True),
    )
    arrived = arrived.reshape(quarter, width)
    placed = arrived[jnp.argsort(arrived_slots.reshape(quarter))]
    own_rows = lax.all_gather(placed, "rep", axis=0, tiled=True)
    share = block_count // copies
    spacing = 1
    rep_position = lax.axis_index("rep")
    travel = (own_rows, value_probe, grad_probe)
    for bit_level in range(copies.bit_length() - 1):
        moved = jax.tree.map(
            lambda part, own: part.astype(own.dtype),
            passed_along(shortened(travel), "blk", share * (1 << bit_level)),
            travel,
        )
        chosen = rep_position // (1 << bit_level) % 2 == 1
        travel = tuple((jnp.where(chosen, fresh, stale) for fresh, stale in zip(moved, travel)))
    totals = (
        jnp.zeros((block_rows, probes), jnp.float32),
        jnp.zeros((block_rows, probes * width), jnp.float32),
    )

    def turn_single(step_index, carry):
        near_part, sums_now = carry
        sums_now = pair_terms(own_rows, near_part, scaling, sums_now)
        near_part = jax.tree.map(
            lambda part, own: part.astype(own.dtype),
            passed_along(shortened(near_part), "blk", spacing),
            near_part,
        )
        return (near_part, sums_now)

    travel, totals = lax.fori_loop(0, share - 1, turn_single, (travel, totals))
    totals = pair_terms(own_rows, travel, scaling, totals)
    values, grads = totals
    value_out, grad_out = (
        lax.psum_scatter(values.T, "rep", scatter_dimension=1, tiled=True),
        lax.psum_scatter(grads, "rep", scatter_dimension=0, tiled=True),
    )
    return (value_out, grad_out)


def solution(mesh):
    placed = (P(("blk", "rep"), None), P(("blk", "rep")), P(None, "blk"), P("blk", None))
    return jax.shard_map(
        per_device,
        mesh=mesh,
        in_specs=placed,
        out_specs=(P(None, ("blk", "rep")), P(("blk", "rep"), None)),
        check_vma=False,
    )
```

profile of v0, /device:TPU:1, one launch (start us, length us, event | category | flops | bytes accessed | tf_op | source)
XLA Modules:
  0.0 380.3 jit_solution(4479877753234815094)
XLA Ops:
  15.5 10.1 %all-to-all-start.1 = ((s32[32,1,4]{2,1,0:T(1,128)}), s32[32,1,4]{2,1,0:T(1,128)S(1)}, u32[]{:S(2)}, u32[]{:S(2)}) async-start(s32[32,1,4]{2,1,0:T(1,128)} %bitcast.2), calls=%async_computation.1 | async-start | bytes 32768 | tf_op jit(solution)/shard_map/all_to_all | solution.py:67
  28.2 7.4 %all-to-all-done.1 = s32[32,1,4]{2,1,0:T(1,128)S(1)} async-done(((s32[32,1,4]{2,1,0:T(1,128)}), s32[32,1,4]{2,1,0:T(1,128)S(1)}, u32[]{:S(2)}, u32[]{:S(2)}) %all-to-all-start.1) | async-done | bytes 544 | tf_op jit(solution)/shard_map/all_to_all | solution.py:67
  35.6 7.3 %all-to-all-start = ((bf16[32,4,128]{2,1,0:T(4,128)(2,1)}), bf16[32,4,128]{2,1,0:T(4,128)(2,1)S(1)}, u32[]{:S(2)}, u32[]{:S(2)}) async-start(bf16[32,4,128]{2,1,0:T(4,128)(2,1)} %bitcast), calls=%async_computation | async-start | bytes 65536 | tf_op jit(solution)/shard_map/all_to_all | solution.py:66
  52.4 8.8 %all-gather = bf16[512,128]{1,0:T(8,128)(2,1)} all-gather(bf16[128,128]{1,0:T(8,128)(2,1)S(1)} %gather_fusion.2), channel_id=2, replica_groups=mesh['blk'=32,'rep'=4] {'rep'}, dimensions={0}, use_global_device_ids=true | all-gather | bytes 163840 | tf_op jit(solution)/shard_map/all_gather | solution.py:71
  61.9 8.8 %collective-permute-done.6 = bf16[8,512]{1,0:T(8,128)(2,1)S(1)} collective-permute-done((bf16[8,512]{1,0:T(8,128)(2,1)S(1)}, bf16[8,512]{1,0:T(8,128)(2,1)S(1)}, u32[]{:S(2)}, u32[]{:S(2)}) %collective-permute-start.6) | collective-permute-done | bytes 8224 | tf_op jit(solution)/shard_map/ppermute | solution.py:14
  70.6 6.3 %collective-permute-done.3 = bf16[512,128]{1,0:T(8,128)(2,1)S(1)} collective-permute-done((bf16[512,128]{1,0:T(8,128)(2,1)}, bf16[512,128]{1,0:T(8,128)(2,1)S(1)}, u32[]{:S(2)}, u32[]{:S(2)}) %collective-permute-start.3) | collective-permute-done | bytes 131104 | tf_op jit(solution)/shard_map/ppermute | solution.py:14
  84.3 216.9 %while.19 = (s32[]{:T(128)}, bf16[512,128]{1,0:T(8,128)(2,1)}, bf16[8,512]{1,0:T(8,128)(2,1)S(1)}, bf16[512,1024]{1,0:T(8,128)(2,1)}, f32[512,8]{0,1:T(8,128)S(1...) while((s32[]{:T(128)}, bf16[512,128]{1,0:T(8,128)(2,1)}, ...), condition=%wide.region_6.7_spmd.clone, body=%wide.region_2.6_spmd.clone.sunk | while | flops 1696280576 | bytes 63365424 | solution.py:99
  94.9 3.6 fusion.76
  98.5 4.7 %convolution_multiply_fusion.5 = f32[4096,128]{1,0:T(8,128)} fusion(bf16[512,128]{1,0:T(8,128)(2,1)} %copy.80, bf16[512,8,512]{2,0,1:T(8,128)(2,1)S(1)} %get-tuple-element.153), kind=kOutput, calls=%fused_computation.8.clone.1 | convolution fusion | flops 537395200 | bytes 6422528 | tf_op jit(solution)/shard_map/while/body/eval_jaxpr/dot_general | solution.py:43
  111.6 7.8 %collective-permute-done.2 = bf16[512,1024]{1,0:T(8,128)(2,1)} collective-permute-done((bf16[512,1024]{1,0:T(8,128)(2,1)S(1)}, bf16[512,1024]{1,0:T(8,128)(2,1)}, u32[]{:S(2)}, u32[]{:S(2)}) %collective-permute-start.2) | collective-permute-done | bytes 1048608 | tf_op jit(solution)/shard_map/while/body/eval_jaxpr/ppermute | solution.py:14
  126.7 3.6 fusion.76
  130.3 4.7 %convolution_multiply_fusion.5 = f32[4096,128]{1,0:T(8,128)} fusion(bf16[512,128]{1,0:T(8,128)(2,1)} %copy.80, bf16[512,8,512]{2,0,1:T(8,128)(2,1)S(1)} %get-tuple-element.153), kind=kOutput, calls=%fused_computation.8.clone.1 | convolution fusion | flops 537395200 | bytes 6422528 | tf_op jit(solution)/shard_map/while/body/eval_jaxpr/dot_general | solution.py:43
  143.5 8.3 %collective-permute-done.2 = bf16[512,1024]{1,0:T(8,128)(2,1)} collective-permute-done((bf16[512,1024]{1,0:T(8,128)(2,1)S(1)}, bf16[512,1024]{1,0:T(8,128)(2,1)}, u32[]{:S(2)}, u32[]{:S(2)}) %collective-permute-start.2) | collective-permute-done | bytes 1048608 | tf_op jit(solution)/shard_map/while/body/eval_jaxpr/ppermute | solution.py:14
  159.1 3.6 fusion.76
  162.7 4.7 %convolution_multiply_fusion.5 = f32[4096,128]{1,0:T(8,128)} fusion(bf16[512,128]{1,0:T(8,128)(2,1)} %copy.80, bf16[512,8,512]{2,0,1:T(8,128)(2,1)S(1)} %get-tuple-element.153), kind=kOutput, calls=%fused_computation.8.clone.1 | convolution fusion | flops 537395200 | bytes 6422528 | tf_op jit(solution)/shard_map/while/body/eval_jaxpr/dot_general | solution.py:43
  175.8 7.5 %collective-permute-done.2 = bf16[512,1024]{1,0:T(8,128)(2,1)} collective-permute-done((bf16[512,1024]{1,0:T(8,128)(2,1)S(1)}, bf16[512,1024]{1,0:T(8,128)(2,1)}, u32[]{:S(2)}, u32[]{:S(2)}) %collective-permute-start.2) | collective-permute-done | bytes 1048608 | tf_op jit(solution)/shard_map/while/body/eval_jaxpr/ppermute | solution.py:14
  190.7 3.6 fusion.76
  194.3 4.7 %convolution_multiply_fusion.5 = f32[4096,128]{1,0:T(8,128)} fusion(bf16[512,128]{1,0:T(8,128)(2,1)} %copy.80, bf16[512,8,512]{2,0,1:T(8,128)(2,1)S(1)} %get-tuple-element.153), kind=kOutput, calls=%fused_computation.8.clone.1 | convolution fusion | flops 537395200 | bytes 6422528 | tf_op jit(solution)/shard_map/while/body/eval_jaxpr/dot_general | solution.py:43
  207.4 6.6 %collective-permute-done.2 = bf16[512,1024]{1,0:T(8,128)(2,1)} collective-permute-done((bf16[512,1024]{1,0:T(8,128)(2,1)S(1)}, bf16[512,1024]{1,0:T(8,128)(2,1)}, u32[]{:S(2)}, u32[]{:S(2)}) %collective-permute-start.2) | collective-permute-done | bytes 1048608 | tf_op jit(solution)/shard_map/while/body/eval_jaxpr/ppermute | solution.py:14
  221.4 3.6 fusion.76
  225.0 4.7 %convolution_multiply_fusion.5 = f32[4096,128]{1,0:T(8,128)} fusion(bf16[512,128]{1,0:T(8,128)(2,1)} %copy.80, bf16[512,8,512]{2,0,1:T(8,128)(2,1)S(1)} %get-tuple-element.153), kind=kOutput, calls=%fused_computation.8.clone.1 | convolution fusion | flops 537395200 | bytes 6422528 | tf_op jit(solution)/shard_map/while/body/eval_jaxpr/dot_general | solution.py:43
  238.1 5.8 %collective-permute-done.2 = bf16[512,1024]{1,0:T(8,128)(2,1)} collective-permute-done((bf16[512,1024]{1,0:T(8,128)(2,1)S(1)}, bf16[512,1024]{1,0:T(8,128)(2,1)}, u32[]{:S(2)}, u32[]{:S(2)}) %collective-permute-start.2) | collective-permute-done | bytes 1048608 | tf_op jit(solution)/shard_map/while/body/eval_jaxpr/ppermute | solution.py:14
  251.3 3.6 fusion.76
  254.9 4.7 %convolution_multiply_fusion.5 = f32[4096,128]{1,0:T(8,128)} fusion(bf16[512,128]{1,0:T(8,128)(2,1)} %copy.80, bf16[512,8,512]{2,0,1:T(8,128)(2,1)S(1)} %get-tuple-element.153), kind=kOutput, calls=%fused_computation.8.clone.1 | convolution fusion | flops 537395200 | bytes 6422528 | tf_op jit(solution)/shard_map/while/body/eval_jaxpr/dot_general | solution.py:43
  268.0 5.0 %collective-permute-done.2 = bf16[512,1024]{1,0:T(8,128)(2,1)} collective-permute-done((bf16[512,1024]{1,0:T(8,128)(2,1)S(1)}, bf16[512,1024]{1,0:T(8,128)(2,1)}, u32[]{:S(2)}, u32[]{:S(2)}) %collective-permute-start.2) | collective-permute-done | bytes 1048608 | tf_op jit(solution)/shard_map/while/body/eval_jaxpr/ppermute | solution.py:14
  280.4 3.6 fusion.76
  284.0 4.7 %convolution_multiply_fusion.5 = f32[4096,128]{1,0:T(8,128)} fusion(bf16[512,128]{1,0:T(8,128)(2,1)} %copy.80, bf16[512,8,512]{2,0,1:T(8,128)(2,1)S(1)} %get-tuple-element.153), kind=kOutput, calls=%fused_computation.8.clone.1 | convolution fusion | flops 537395200 | bytes 6422528 | tf_op jit(solution)/shard_map/while/body/eval_jaxpr/dot_general | solution.py:43
  297.1 4.1 %collective-permute-done.2 = bf16[512,1024]{1,0:T(8,128)(2,1)} collective-permute-done((bf16[512,1024]{1,0:T(8,128)(2,1)S(1)}, bf16[512,1024]{1,0:T(8,128)(2,1)}, u32[]{:S(2)}, u32[]{:S(2)}) %collective-permute-start.2) | collective-permute-done | bytes 1048608 | tf_op jit(solution)/shard_map/while/body/eval_jaxpr/ppermute | solution.py:14
  313.5 3.4 convolution_multiply_fusion.2
  320.0 4.8 %bitcast_subtract_fusion.3 = f32[512,1024]{1,0:T(8,128)} fusion(f32[64,8,8,128]{3,2,1,0:T(8,128)S(1)} %bitcast.130, f32[512,1024]{1,0:T(8,128)} %mul.165, f32[512,1024]{1,0:T(8,128)S(1)} %copy-done.3, f32[512,1024]{1,0:T(8,128)} %fusion.31), kind=kLoop, calls=%fused_computation.43 | loop fusion | flops 1572864 | bytes 10485760 | tf_op jit(solution)/shard_map/sub | solution.py:50
  324.9 16.4 %reduce-scatter.3.cloned.1.call-done = f32[8,128]{1,0:T(8,128)} async-done(((f32[8,512]{1,0:T(8,128)}), f32[8,128]{1,0:T(8,128)}) %reduce-scatter.3.cloned.1.call-update) | async-done | bytes 4112 | tf_op jit(solution)/shard_map/reduce_scatter | solution.py:103
  341.3 32.1 %reduce-scatter.5.cloned.1.call-done = f32[128,1024]{1,0:T(8,128)} async-done(((f32[512,1024]{1,0:T(8,128)}), f32[128,1024]{1,0:T(8,128)}) %reduce-scatter.5.cloned.1.call-update) | async-done | bytes 524304 | tf_op jit(solution)/shard_map/reduce_scatter | solution.py:104
  (258 shorter events, 156.4 us)
Async XLA Ops:
  7.2 39.7 %collective-permute-start.7 = (bf16[512,1024]{1,0:T(8,128)(2,1)}, bf16[512,1024]{1,0:T(8,128)(2,1)S(1)}, u32[]{:S(2)}, u32[]{:S(2)}) collective-permute-start(bf16[512,1024]{1,0:T(8,128)(2,1)} %param.9), channel_id=1, source_target_pairs={{96,0},{100,4},{104,8},{108,12},{112,16},{116,20},{120,24},{124,28... | collective-permute-start | bytes 3145736 | tf_op jit(solution)/shard_map/ppermute | solution.py:14
  13.6 36.3 %copy-start.6 = (bf16[8,512]{1,0:T(8,128)(2,1)S(1)}, bf16[8,512]{1,0:T(8,128)(2,1)}, u32[]{:S(2)}) copy-start(bf16[8,512]{1,0:T(8,128)(2,1)} %param.8) | copy-start | bytes 24580
  15.5 20.1 %all-to-all-start.1 = ((s32[32,1,4]{2,1,0:T(1,128)}), s32[32,1,4]{2,1,0:T(1,128)S(1)}, u32[]{:S(2)}, u32[]{:S(2)}) async-start(s32[32,1,4]{2,1,0:T(1,128)} %bitcast.2), calls=%async_computation.1 | async-start | bytes 32768 | tf_op jit(solution)/shard_map/all_to_all | solution.py:67
  25.6 24.3 %collective-permute-start.5 = (bf16[8,512]{1,0:T(8,128)(2,1)}, bf16[8,512]{1,0:T(8,128)(2,1)S(1)}, u32[]{:S(2)}, u32[]{:S(2)}) collective-permute-start(bf16[8,512]{1,0:T(8,128)(2,1)} %param.8), channel_id=1, source_target_pairs={{96,0},{100,4},{104,8},{108,12},{112,16},{116,20},{120,24},{124,28... | collective-permute-start | bytes 24584 | tf_op jit(solution)/shard_map/ppermute | solution.py:14
  35.6 16.1 %all-to-all-start = ((bf16[32,4,128]{2,1,0:T(4,128)(2,1)}), bf16[32,4,128]{2,1,0:T(4,128)(2,1)S(1)}, u32[]{:S(2)}, u32[]{:S(2)}) async-start(bf16[32,4,128]{2,1,0:T(4,128)(2,1)} %bitcast), calls=%async_computation | async-start | bytes 65536 | tf_op jit(solution)/shard_map/all_to_all | solution.py:66
  43.0 298.3 %reduce-scatter.3.cloned.1.call-start = ((), (), s32[]{:S(2)}) async-start(), calls=%async_computation.4 | async-start | bytes 20480 | tf_op jit(solution)/shard_map/reduce_scatter | solution.py:103
  47.0 36.1 %collective-permute-start.8 = (bf16[512,1024]{1,0:T(8,128)(2,1)S(1)}, bf16[512,1024]{1,0:T(8,128)(2,1)S(1)}, u32[]{:S(2)}, u32[]{:S(2)}) collective-permute-start(bf16[512,1024]{1,0:T(8,128)(2,1)S(1)} %broadcast_select_fusion), channel_id=1, source_target_pairs={{64,0},{68,4},{72,8},{76,12},{80,16},{84,20},{88,24},{92,28},{96,3... | collective-permute-start | bytes 3145736 | tf_op jit(solution)/shard_map/ppermute | solution.py:14
  49.9 20.8 %collective-permute-start.6 = (bf16[8,512]{1,0:T(8,128)(2,1)S(1)}, bf16[8,512]{1,0:T(8,128)(2,1)S(1)}, u32[]{:S(2)}, u32[]{:S(2)}) collective-permute-start(bf16[8,512]{1,0:T(8,128)(2,1)S(1)} %broadcast_select_fusion.4), channel_id=1, source_target_pairs={{64,0},{68,4},{72,8},{76,12},{80,16},{84,20},{88,24},{92,28},{96,3... | collective-permute-start | bytes 24584 | tf_op jit(solution)/shard_map/ppermute | solution.py:14
  61.3 15.6 %collective-permute-start.3 = (bf16[512,128]{1,0:T(8,128)(2,1)}, bf16[512,128]{1,0:T(8,128)(2,1)S(1)}, u32[]{:S(2)}, u32[]{:S(2)}) collective-permute-start(bf16[512,128]{1,0:T(8,128)(2,1)} %all-gather), channel_id=1, source_target_pairs={{96,0},{100,4},{104,8},{108,12},{112,16},{116,20},{120,24},{124,28... | collective-permute-start | bytes 393224 | tf_op jit(solution)/shard_map/ppermute | solution.py:14
  76.9 5.6 %collective-permute-start.4 = (bf16[512,128]{1,0:T(8,128)(2,1)S(1)}, bf16[512,128]{1,0:T(8,128)(2,1)S(1)}, u32[]{:S(2)}, u32[]{:S(2)}) collective-permute-start(bf16[512,128]{1,0:T(8,128)(2,1)S(1)} %broadcast_select_fusion.2), channel_id=1, source_target_pairs={{64,0},{68,4},{72,8},{76,12},{80,16},{84,20},{88,24},{92,28},{96,3... | collective-permute-start | bytes 393224 | tf_op jit(solution)/shard_map/ppermute | solution.py:14
  84.3 27.3 %collective-permute-start.1 = (bf16[8,512]{1,0:T(8,128)(2,1)S(1)}, bf16[8,512]{1,0:T(8,128)(2,1)S(1)}, u32[]{:S(2)}, u32[]{:S(2)}) collective-permute-start(bf16[8,512]{1,0:T(8,128)(2,1)S(1)} %copy.81), channel_id=1, source_target_pairs={{124,0},{0,4},{4,8},{8,12},{12,16},{16,20},{20,24},{24,28},{28,32}... | collective-permute-start | bytes 24584 | tf_op jit(solution)/shard_map/while/body/eval_jaxpr/ppermute | solution.py:14
  87.0 24.6 %collective-permute-start = (bf16[512,128]{1,0:T(8,128)(2,1)}, bf16[512,128]{1,0:T(8,128)(2,1)}, u32[]{:S(2)}, u32[]{:S(2)}) collective-permute-start(bf16[512,128]{1,0:T(8,128)(2,1)} %copy.80), channel_id=1, source_target_pairs={{124,0},{0,4},{4,8},{8,12},{12,16},{16,20},{20,24},{24,28},{28,32}... | collective-permute-start | bytes 393224 | tf_op jit(solution)/shard_map/while/body/eval_jaxpr/ppermute | solution.py:14
  89.4 30.0 %collective-permute-start.2 = (bf16[512,1024]{1,0:T(8,128)(2,1)S(1)}, bf16[512,1024]{1,0:T(8,128)(2,1)}, u32[]{:S(2)}, u32[]{:S(2)}) collective-permute-start(bf16[512,1024]{1,0:T(8,128)(2,1)S(1)} %copy.82), channel_id=1, source_target_pairs={{124,0},{0,4},{4,8},{8,12},{12,16},{16,20},{20,24},{24,28},{28,32}... | collective-permute-start | bytes 3145736 | tf_op jit(solution)/shard_map/while/body/eval_jaxpr/ppermute | solution.py:14
  119.4 24.1 %collective-permute-start.1 = (bf16[8,512]{1,0:T(8,128)(2,1)S(1)}, bf16[8,512]{1,0:T(8,128)(2,1)S(1)}, u32[]{:S(2)}, u32[]{:S(2)}) collective-permute-start(bf16[8,512]{1,0:T(8,128)(2,1)S(1)} %copy.81), channel_id=1, source_target_pairs={{124,0},{0,4},{4,8},{8,12},{12,16},{16,20},{20,24},{24,28},{28,32}... | collective-permute-start | bytes 24584 | tf_op jit(solution)/shard_map/while/body/eval_jaxpr/ppermute | solution.py:14
  120.9 22.5 %collective-permute-start = (bf16[512,128]{1,0:T(8,128)(2,1)}, bf16[512,128]{1,0:T(8,128)(2,1)}, u32[]{:S(2)}, u32[]{:S(2)}) collective-permute-start(bf16[512,128]{1,0:T(8,128)(2,1)} %copy.80), channel_id=1, source_target_pairs={{124,0},{0,4},{4,8},{8,12},{12,16},{16,20},{20,24},{24,28},{28,32}... | collective-permute-start | bytes 393224 | tf_op jit(solution)/shard_map/while/body/eval_jaxpr/ppermute | solution.py:14
  122.2 29.6 %collective-permute-start.2 = (bf16[512,1024]{1,0:T(8,128)(2,1)S(1)}, bf16[512,1024]{1,0:T(8,128)(2,1)}, u32[]{:S(2)}, u32[]{:S(2)}) collective-permute-start(bf16[512,1024]{1,0:T(8,128)(2,1)S(1)} %copy.82), channel_id=1, source_target_pairs={{124,0},{0,4},{4,8},{8,12},{12,16},{16,20},{20,24},{24,28},{28,32}... | collective-permute-start | bytes 3145736 | tf_op jit(solution)/shard_map/while/body/eval_jaxpr/ppermute | solution.py:14
  151.8 24.1 %collective-permute-start.1 = (bf16[8,512]{1,0:T(8,128)(2,1)S(1)}, bf16[8,512]{1,0:T(8,128)(2,1)S(1)}, u32[]{:S(2)}, u32[]{:S(2)}) collective-permute-start(bf16[8,512]{1,0:T(8,128)(2,1)S(1)} %copy.81), channel_id=1, source_target_pairs={{124,0},{0,4},{4,8},{8,12},{12,16},{16,20},{20,24},{24,28},{28,32}... | collective-permute-start | bytes 24584 | tf_op jit(solution)/shard_map/while/body/eval_jaxpr/ppermute | solution.py:14
  153.3 22.5 %collective-permute-start = (bf16[512,128]{1,0:T(8,128)(2,1)}, bf16[512,128]{1,0:T(8,128)(2,1)}, u32[]{:S(2)}, u32[]{:S(2)}) collective-permute-start(bf16[512,128]{1,0:T(8,128)(2,1)} %copy.80), channel_id=1, source_target_pairs={{124,0},{0,4},{4,8},{8,12},{12,16},{16,20},{20,24},{24,28},{28,32}... | collective-permute-start | bytes 393224 | tf_op jit(solution)/shard_map/while/body/eval_jaxpr/ppermute | solution.py:14
  154.6 28.8 %collective-permute-start.2 = (bf16[512,1024]{1,0:T(8,128)(2,1)S(1)}, bf16[512,1024]{1,0:T(8,128)(2,1)}, u32[]{:S(2)}, u32[]{:S(2)}) collective-permute-start(bf16[512,1024]{1,0:T(8,128)(2,1)S(1)} %copy.82), channel_id=1, source_target_pairs={{124,0},{0,4},{4,8},{8,12},{12,16},{16,20},{20,24},{24,28},{28,32}... | collective-permute-start | bytes 3145736 | tf_op jit(solution)/shard_map/while/body/eval_jaxpr/ppermute | solution.py:14
  183.3 24.1 %collective-permute-start.1 = (bf16[8,512]{1,0:T(8,128)(2,1)S(1)}, bf16[8,512]{1,0:T(8,128)(2,1)S(1)}, u32[]{:S(2)}, u32[]{:S(2)}) collective-permute-start(bf16[8,512]{1,0:T(8,128)(2,1)S(1)} %copy.81), channel_id=1, source_target_pairs={{124,0},{0,4},{4,8},{8,12},{12,16},{16,20},{20,24},{24,28},{28,32}... | collective-permute-start | bytes 24584 | tf_op jit(solution)/shard_map/while/body/eval_jaxpr/ppermute | solution.py:14
  184.9 22.5 %collective-permute-start = (bf16[512,128]{1,0:T(8,128)(2,1)}, bf16[512,128]{1,0:T(8,128)(2,1)}, u32[]{:S(2)}, u32[]{:S(2)}) collective-permute-start(bf16[512,128]{1,0:T(8,128)(2,1)} %copy.80), channel_id=1, source_target_pairs={{124,0},{0,4},{4,8},{8,12},{12,16},{16,20},{20,24},{24,28},{28,32}... | collective-permute-start | bytes 393224 | tf_op jit(solution)/shard_map/while/body/eval_jaxpr/ppermute | solution.py:14
  186.1 27.9 %collective-permute-start.2 = (bf16[512,1024]{1,0:T(8,128)(2,1)S(1)}, bf16[512,1024]{1,0:T(8,128)(2,1)}, u32[]{:S(2)}, u32[]{:S(2)}) collective-permute-start(bf16[512,1024]{1,0:T(8,128)(2,1)S(1)} %copy.82), channel_id=1, source_target_pairs={{124,0},{0,4},{4,8},{8,12},{12,16},{16,20},{20,24},{24,28},{28,32}... | collective-permute-start | bytes 3145736 | tf_op jit(solution)/shard_map/while/body/eval_jaxpr/ppermute | solution.py:14
  214.1 24.1 %collective-permute-start.1 = (bf16[8,512]{1,0:T(8,128)(2,1)S(1)}, bf16[8,512]{1,0:T(8,128)(2,1)S(1)}, u32[]{:S(2)}, u32[]{:S(2)}) collective-permute-start(bf16[8,512]{1,0:T(8,128)(2,1)S(1)} %copy.81), channel_id=1, source_target_pairs={{124,0},{0,4},{4,8},{8,12},{12,16},{16,20},{20,24},{24,28},{28,32}... | collective-permute-start | bytes 24584 | tf_op jit(solution)/shard_map/while/body/eval_jaxpr/ppermute | solution.py:14
  215.6 22.5 %collective-permute-start = (bf16[512,128]{1,0:T(8,128)(2,1)}, bf16[512,128]{1,0:T(8,128)(2,1)}, u32[]{:S(2)}, u32[]{:S(2)}) collective-permute-start(bf16[512,128]{1,0:T(8,128)(2,1)} %copy.80), channel_id=1, source_target_pairs={{124,0},{0,4},{4,8},{8,12},{12,16},{16,20},{20,24},{24,28},{28,32}... | collective-permute-start | bytes 393224 | tf_op jit(solution)/shard_map/while/body/eval_jaxpr/ppermute | solution.py:14
  216.8 27.1 %collective-permute-start.2 = (bf16[512,1024]{1,0:T(8,128)(2,1)S(1)}, bf16[512,1024]{1,0:T(8,128)(2,1)}, u32[]{:S(2)}, u32[]{:S(2)}) collective-permute-start(bf16[512,1024]{1,0:T(8,128)(2,1)S(1)} %copy.82), channel_id=1, source_target_pairs={{124,0},{0,4},{4,8},{8,12},{12,16},{16,20},{20,24},{24,28},{28,32}... | collective-permute-start | bytes 3145736 | tf_op jit(solution)/shard_map/while/body/eval_jaxpr/ppermute | solution.py:14
  243.9 24.1 %collective-permute-start.1 = (bf16[8,512]{1,0:T(8,128)(2,1)S(1)}, bf16[8,512]{1,0:T(8,128)(2,1)S(1)}, u32[]{:S(2)}, u32[]{:S(2)}) collective-permute-start(bf16[8,512]{1,0:T(8,128)(2,1)S(1)} %copy.81), channel_id=1, source_target_pairs={{124,0},{0,4},{4,8},{8,12},{12,16},{16,20},{20,24},{24,28},{28,32}... | collective-permute-start | bytes 24584 | tf_op jit(solution)/shard_map/while/body/eval_jaxpr/ppermute | solution.py:14
  245.5 22.5 %collective-permute-start = (bf16[512,128]{1,0:T(8,128)(2,1)}, bf16[512,128]{1,0:T(8,128)(2,1)}, u32[]{:S(2)}, u32[]{:S(2)}) collective-permute-start(bf16[512,128]{1,0:T(8,128)(2,1)} %copy.80), channel_id=1, source_target_pairs={{124,0},{0,4},{4,8},{8,12},{12,16},{16,20},{20,24},{24,28},{28,32}... | collective-permute-start | bytes 393224 | tf_op jit(solution)/shard_map/while/body/eval_jaxpr/ppermute | solution.py:14
  246.7 26.3 %collective-permute-start.2 = (bf16[512,1024]{1,0:T(8,128)(2,1)S(1)}, bf16[512,1024]{1,0:T(8,128)(2,1)}, u32[]{:S(2)}, u32[]{:S(2)}) collective-permute-start(bf16[512,1024]{1,0:T(8,128)(2,1)S(1)} %copy.82), channel_id=1, source_target_pairs={{124,0},{0,4},{4,8},{8,12},{12,16},{16,20},{20,24},{24,28},{28,32}... | collective-permute-start | bytes 3145736 | tf_op jit(solution)/shard_map/while/body/eval_jaxpr/ppermute | solution.py:14
  273.0 24.1 %collective-permute-start.1 = (bf16[8,512]{1,0:T(8,128)(2,1)S(1)}, bf16[8,512]{1,0:T(8,128)(2,1)S(1)}, u32[]{:S(2)}, u32[]{:S(2)}) collective-permute-start(bf16[8,512]{1,0:T(8,128)(2,1)S(1)} %copy.81), channel_id=1, source_target_pairs={{124,0},{0,4},{4,8},{8,12},{12,16},{16,20},{20,24},{24,28},{28,32}... | collective-permute-start | bytes 24584 | tf_op jit(solution)/shard_map/while/body/eval_jaxpr/ppermute | solution.py:14
  274.6 22.5 %collective-permute-start = (bf16[512,128]{1,0:T(8,128)(2,1)}, bf16[512,128]{1,0:T(8,128)(2,1)}, u32[]{:S(2)}, u32[]{:S(2)}) collective-permute-start(bf16[512,128]{1,0:T(8,128)(2,1)} %copy.80), channel_id=1, source_target_pairs={{124,0},{0,4},{4,8},{8,12},{12,16},{16,20},{20,24},{24,28},{28,32}... | collective-permute-start | bytes 393224 | tf_op jit(solution)/shard_map/while/body/eval_jaxpr/ppermute | solution.py:14
  275.8 25.4 %collective-permute-start.2 = (bf16[512,1024]{1,0:T(8,128)(2,1)S(1)}, bf16[512,1024]{1,0:T(8,128)(2,1)}, u32[]{:S(2)}, u32[]{:S(2)}) collective-permute-start(bf16[512,1024]{1,0:T(8,128)(2,1)S(1)} %copy.82), channel_id=1, source_target_pairs={{124,0},{0,4},{4,8},{8,12},{12,16},{16,20},{20,24},{24,28},{28,32}... | collective-permute-start | bytes 3145736 | tf_op jit(solution)/shard_map/while/body/eval_jaxpr/ppermute | solution.py:14
  319.2 54.2 %reduce-scatter.5.cloned.1.call-start = ((), (), s32[]{:S(2)}) async-start(), calls=%async_computation.5 | async-start | bytes 2621440 | tf_op jit(solution)/shard_map/reduce_scatter | solution.py:104
  (24 other events, 70.2 us)
Sparse Core Ops, SparseCore 0:
  319.3 21.9 reduce-scatter.2
  344.4 28.9 reduce-scatter.4
where the time goes:
time: 383 us; the launch traced here: 380 us
  waiting for transfers between devices  119 us (31%)
  matrix products  111 us (29%)
  local copies, waits for them, and re-layouts  57.6 us (15%)
  other arithmetic  38.1 us (10%)
  starting transfers between devices  31.2 us (8%)
  between operations  14.2 us (4%)
  blocking collectives  8.84 us (2%)
    ppermute x27, waiting for transfers between devices, passed_along(): return lax.ppermute(block, axis, route)  61.3 us
    dot_general x8, matrix products, pair_terms(): jnp.dot(coef_low, col_rows, preferred_element_type=jnp.float32)  36.6 us
    reduce_scatter x1, waiting for transfers between devices, per_device(): lax.psum_scatter(grads, 'rep', scatter_dimension=0, tiled=True)  32.1 us
    while x70, local copies, waits for them, and re-layouts  30.9 us
    dot_general x8, matrix products, pair_terms(): jnp.einsum('id,jpd->ipj', own_rows, shaped, preferred_element_type=jnp.fl...  28.4 us
    dot_general x8, matrix products, pair_terms(): jnp.dot(kernel.astype(jnp.bfloat16), col_grads, preferred_element_type=jn...  22.1 us
    reduce_scatter x1, waiting for transfers between devices, per_device(): lax.psum_scatter(values.T, 'rep', scatter_dimension=1, tiled=True)  16.4 us
    ppermute x27, starting transfers between devices, passed_along(): return lax.ppermute(block, axis, route)  13.7 us
  transfers between devices with their start and end apart: 31, of which 14 were waited for; matrix products, arithmetic and copies ran while one was open for 47% of the time, Pallas kernels for 0%

commit v1 on v0

v1 whole, which is shorter than its diff:
```python
import functools

import jax
import jax.numpy as jnp
from jax import lax
from jax.experimental import pallas as pl
from jax.experimental.pallas import tpu as pltpu
from jax.sharding import PartitionSpec as P

F32, BF16 = jnp.float32, jnp.bfloat16
MESH = pl.DeviceIdType.MESH
LOG2E = 1.4426950408889634
WIRE = BF16

SLOTS = (
    (0, 0), (1, 0), (3, 0), (0, 1),
    (0, 3), (2, 0), (0, 2), (1, 1),
    (1, 3), (3, 1), (3, 3), (2, 1), (2, 3), (1, 2), (3, 2), (2, 2),
)
NEAR = ((1, 0), (3, 0), (0, 1), (0, 3))
SECOND = ((2, 0), (1, 1), (3, 3), (1, 3), (3, 1), (0, 2))
THIRD = ((2, 1), (2, 3), (1, 2), (3, 2))
LAST = ((2, 2),)


def nt(a, b):
    return lax.dot_general(a, b, (((1,), (1,)), ((), ())), preferred_element_type=F32)


def nn(a, b):
    return jnp.dot(a, b, preferred_element_type=F32)


def split3(a):
    hi = a.astype(BF16)
    rest = a - hi.astype(F32)
    mid = rest.astype(BF16)
    return hi, mid, (rest - mid.astype(F32)).astype(BF16)


def kernel(
    feat, row_r, row_c, vprobe, gprobe, vout, gout,
    M, N, G, Z, W, OWN, BI, X, V, KB, KS, DB, PB, VIA, RX, VS, VR,
    a2a_s, a2a_r, own_s, own_r, loc, g_s, g_r, z_s, z_r, d_s, d_r, y_s, via_r, rx_r, v_s, v_r,
):
    rho = 512.0 ** -0.25
    c1 = rho * rho * LOG2E
    b, r = lax.axis_index("blk"), lax.axis_index("rep")
    x, z = b % 4, b // 8
    y, core = (b // 4) % 2 * 2 + r // 2, r % 2

    def at_xz(dx, dz):
        return ((z + dz) % 4 * 8 + b // 4 % 2 * 4 + (x + dx) % 4, r)

    def at_y(dy, dc):
        yy = (y + dy) % 4
        return (z * 8 + yy // 2 * 4 + x, yy % 2 * 2 + (core + dc) % 2)

    def remote(src, dst, ss, rs, dev):
        return pltpu.make_async_remote_copy(
            src_ref=src, dst_ref=dst, send_sem=ss, recv_sem=rs, device_id=dev, device_id_type=MESH)

    mine = pltpu.make_async_copy(gprobe.at[pl.ds(pl.multiple_of(r * 128, 128), 128), :], G.at[0], loc)
    mine.start()

    oc, orow = row_c[...], row_r[...]
    rank = jnp.sum((oc < orow).astype(F32), axis=0, keepdims=True)
    q = lax.broadcasted_iota(jnp.int32, (256, 128), 0)
    pick = (rank == (q // 8 * 4 + q % 4).astype(F32)).astype(BF16)
    slot = jnp.broadcast_to((oc % 128).astype(F32), (128, 128)).astype(BF16)
    both = nn(pick, jnp.concatenate([feat[...], slot], axis=1))
    M[...] = jnp.where(q % 8 < 4, both[:, :128], both[:, 128:]).reshape(32, 8, 128)

    barrier = pltpu.get_barrier_semaphore()

    def greet(k, _):
        pl.semaphore_signal(barrier, inc=1, device_id=((b + k) % 32, r), device_id_type=MESH)
        return 0

    lax.fori_loop(1, 32, greet, 0)
    for dy, dc in ((1, 0), (3, 0), (0, 1), (1, 1), (2, 1), (3, 1)):
        pl.semaphore_signal(barrier, inc=1, device_id=at_y(dy, dc), device_id_type=MESH)
    pl.semaphore_wait(barrier, 37)

    def deal(k, _):
        to = (b + k) % 32
        remote(M.at[to], N.at[k], a2a_s, a2a_r, (to, r)).start()
        return 0

    lax.fori_loop(1, 32, deal, 0)
    N[0] = M[b]

    chans = {"g": (G, 64, g_s, g_r), "z": (Z, 80, z_s, z_r)}

    def piece(ch, h, s):
        buf, rows, ss, rs = chans[ch]
        return buf.at[s, pl.ds(h * rows, rows), :]

    def slot_of(h, i1, i2):
        return SLOTS.index((i1 % 4, i2 % 4) if h == 0 else (i2 % 4, i1 % 4))

    def send(ch, h, i1, i2, e1, e2):
        buf, rows, ss, rs = chans[ch]
        t = slot_of(h, i1 + e1, i2 + e2)
        remote(piece(ch, h, slot_of(h, i1, i2)), piece(ch, h, t), ss, rs.at[h, t],
               at_xz(e1, e2) if h == 0 else at_xz(e2, e1)).start()

    def handle(ch, h, i1, i2):
        buf, rows, ss, rs = chans[ch]
        if (i1, i2) != (0, 0):
            s = slot_of(h, i1, i2)
            remote(piece(ch, h, s), piece(ch, h, s), ss, rs.at[h, s], (b, r)).wait_recv()
        if i2 == 0:
            if i1 == 0 or (i1 == 1 and h == 0):
                send(ch, h, i1, 0, 1, 0)
            if i1 == 0 or (i1 == 3 and h == 1):
                send(ch, h, i1, 0, -1, 0)
            send(ch, h, i1, 0, 0, 1)
            send(ch, h, i1, 0, 0, -1)
        if i2 == 1 and i1 in (0, 1):
            send(ch, h, i1, 1, 0, 1)
        if i2 == 3 and i1 in (3, 2):
            send(ch, h, i1, 3, 0, -1)

    def events(ch, items):
        for i1, i2 in items:
            for h in (0, 1):
                handle(ch, h, i1, i2)

    mine.wait()
    events("g", ((0, 0),))

    X[...] = jnp.zeros_like(X)
    V[...] = jnp.zeros_like(V)

    remote(M.at[pl.ds(0, 31)], N.at[pl.ds(1, 31)], a2a_s, a2a_r, (b, r)).wait_recv()
    n2 = N[...].reshape(256, 128)
    marks = n2.T[0:1, :]
    lane = lax.broadcasted_iota(jnp.int32, (128, 256), 1)
    want = lax.broadcasted_iota(jnp.int32, (128, 256), 0).astype(F32)
    put = ((marks == want) & (lane % 8 >= 4)).astype(BF16)
    placed32 = nn(put, pltpu.roll(n2, 4, 0).astype(BF16))
    placed = placed32.astype(BF16)
    Z[0, 0:128, :] = placed
    OWN[896:1024, :] = placed
    for k, dy in enumerate((2, 1, 3, 0)):
        for dc in (1, 0):
            if (dy, dc) != (0, 0):
                at = (2, 1, 3, 0).index((-dy) % 4) * 256 + (0 if dc else 128)
                remote(OWN.at[pl.ds(896, 128), :], OWN.at[pl.ds(at, 128), :], own_s, own_r, at_y(dy, dc)).start()

    rows = []
    for p in range(8):
        rows.append(jnp.sum((placed32 * G[0, :, p * 128:(p + 1) * 128].astype(F32)).T, axis=0, keepdims=True))
    anchor = jnp.concatenate(rows, axis=0)
    vp = vprobe[:, pl.ds(pl.multiple_of(r * 128, 128), 128)].astype(F32)
    w = vp * (1.0 / rho) - anchor
    norm = (0.5 * c1) * jnp.sum((placed32 * placed32).T, axis=0, keepdims=True)
    eight = lax.broadcasted_iota(jnp.int32, (8, 128), 0)
    n_hi, n_mid, n_lo = split3(jnp.broadcast_to(norm, (8, 128)))
    tail = jnp.where(eight == 0, n_hi.astype(F32), jnp.where(
        eight == 1, n_mid.astype(F32), jnp.where(eight == 2, n_lo.astype(F32), 0.0)))
    Z[0, 128:160, :] = jnp.concatenate([part.astype(F32) for part in split3(w)] + [tail], axis=0).astype(BF16)
    events("z", ((0, 0),))

    def unpack(s0, count):
        for s in range(s0, s0 + count):
            aux = Z[s, 128:160, :].astype(F32)
            W[s, 0:8, :] = aux[0:8] + aux[8:16] + aux[16:24]
            W[s, 8:9, :] = aux[24:25] + aux[25:26] + aux[26:27]

    events("g", NEAR)
    remote(OWN.at[pl.ds(0, 896), :], OWN.at[pl.ds(0, 896), :], own_s, own_r, (b, r)).wait_recv()
    wide = OWN[...].astype(F32)
    BI[...] = (0.5 * c1) * jnp.sum(wide * wide, axis=1, keepdims=True)
    events("z", NEAR)
    unpack(0, 4)

    def tile(ii, s0, ns, TI):
        TJ = ns * 128
        zz = Z[pl.ds(s0, ns), 0:128, :].reshape(TJ, 128)
        own = OWN[ii, :]
        bj = jnp.concatenate([W[s0 + q, 8:9, :] for q in range(ns)], axis=1)
        k = jnp.exp2(nt(own, zz) * c1 - BI[ii, :] - bj)
        kbig, klow = (KS[0], KB[0]) if ns == 4 else (KS[1], KB[1])
        kbig[...] = k * rho
        klow[...] = k.astype(BF16)
        for hh in range(4):
            hs = pl.ds(hh * 256, 256)
            X[ii, hs] += nn(klow[...], G[pl.ds(s0, ns), :, hs].reshape(TJ, 256))
            for p in (2 * hh, 2 * hh + 1):
                ps = pl.ds(p * 128, 128)
                inner = nt(own, G[pl.ds(s0, ns), :, ps].reshape(TJ, 128))
                wr = jnp.concatenate([W[s0 + q, p:p + 1, :] for q in range(ns)], axis=1)
                coef = kbig[...] * (inner + wr)
                part = coef[:, 0:128]
                for q in range(1, ns):
                    part = part + coef[:, q * 128:(q + 1) * 128]
                V[p, ii, :] += part
                X[ii, ps] += nn(coef.astype(BF16), zz) * rho

    def early(n, _):
        @pl.when(n == 2)
        def _():
            for ch in ("g", "z"):
                events(ch, SECOND)
            unpack(4, 4)

        @pl.when(n == 3)
        def _():
            for ch in ("g", "z"):
                events(ch, THIRD)

        tile(pl.ds(pl.multiple_of(n % 2 * 512, 512), 512), n // 2 * 4, 4, 512)
        return 0

    lax.fori_loop(0, 4, early, 0)
    for ch in ("g", "z"):
        events(ch, LAST)
    unpack(8, 8)

    def core_swap(k):
        return remote(X.at[pl.ds(pl.multiple_of(k * 256, 256), 128), :], DB.at[k], d_s.at[k], d_r.at[k], at_y(0, 1))

    def merged(k):
        core_swap(k).wait_recv()
        return X[k * 256 + 128:k * 256 + 256, :] + DB[k]

    def via(j):
        half = pl.ds(64 * j, 64)
        return remote(PB.at[0, half, :], VIA.at[j], y_s.at[j], via_r.at[j], at_y(1 - 2 * j, 0))

    def step_y(j):
        return remote(PB.at[1 + j], RX.at[j], y_s.at[2 + j], rx_r.at[j], at_y(1 - 2 * j, 0))

    def late(k, _):
        at = pl.multiple_of(k * 256, 256)
        ii = pl.ds(at, 256)
        tile(ii, 8, 8, 256)
        own = OWN[ii, :].astype(F32) * rho
        lanes = lax.broadcasted_iota(jnp.int32, (256, 128), 1)
        vt = jnp.zeros((256, 128), F32)
        for p in range(8):
            col = jnp.sum(V[p, ii, :], axis=1, keepdims=True)
            X[ii, pl.ds(p * 128, 128)] -= own * col
            vt = jnp.where(lanes == p, col, vt)
        core_swap(k).start()
        dy = (2 + 3 * (k % 2) + (k // 2) * (1 + 2 * (k % 2))) % 4
        VS[2 * k] = vt[0:128].T[0:8]
        VS[2 * k + 1] = vt[128:256].T[0:8]
        remote(VS.at[2 * k], VR.at[2 * k], v_s, v_r, at_y(dy, 1)).start()

        @pl.when(k < 3)
        def _():
            remote(VS.at[2 * k + 1], VR.at[2 * k + 1], v_s, v_r, at_y(dy, 0)).start()

        @pl.when(k == 1)
        def _():
            PB[0] = merged(0).astype(WIRE)
            via(0).start()
            via(1).start()

        @pl.when(k == 2)
        def _():
            via(0).wait_recv()
            whole = merged(1)
            PB[1, 0:64, :] = (whole[0:64] + VIA[0].astype(F32)).astype(WIRE)
            PB[1, 64:128, :] = whole[64:128].astype(WIRE)
            step_y(0).start()

        @pl.when(k == 3)
        def _():
            via(1).wait_recv()
            whole = merged(2)
            PB[2, 0:64, :] = whole[0:64].astype(WIRE)
            PB[2, 64:128, :] = (whole[64:128] + VIA[1].astype(F32)).astype(WIRE)
            step_y(1).start()

        return 0

    lax.fori_loop(0, 4, late, 0)
    total = merged(3)
    remote(VR.at[pl.ds(0, 7)], VR.at[pl.ds(0, 7)], v_s, v_r, (b, r)).wait()
    value = VS[7]
    for j in range(7):
        value = value + VR[j]
    vout[...] = value
    step_y(0).wait_recv()
    step_y(1).wait_recv()
    gout[...] = total + RX[0].astype(F32) + RX[1].astype(F32)

    remote(M.at[pl.ds(0, 31)], N.at[pl.ds(1, 31)], a2a_s, a2a_r, (b, r)).wait_send()
    remote(OWN.at[pl.ds(0, 896), :], OWN.at[pl.ds(0, 896), :], own_s, own_r, (b, r)).wait_send()
    for ch in ("g", "z"):
        buf, _, ss, rs = chans[ch]
        remote(buf.at[pl.ds(0, 15)], buf.at[pl.ds(0, 15)], ss, rs.at[0, 0], (b, r)).wait_send()
    for k in range(4):
        core_swap(k).wait_send()
    for j in (0, 1):
        via(j).wait_send()
        step_y(j).wait_send()


def per_device(features, owner_row, value_probe, grad_probe):
    vmem = pl.BlockSpec(memory_space=pltpu.VMEM)
    dma = pltpu.SemaphoreType.DMA
    return pl.pallas_call(
        kernel,
        out_shape=(jax.ShapeDtypeStruct((8, 128), F32), jax.ShapeDtypeStruct((128, 1024), F32)),
        in_specs=[vmem, vmem, vmem, vmem, pl.BlockSpec(memory_space=pl.ANY)],
        out_specs=(vmem, vmem),
        scratch_shapes=[
            pltpu.VMEM((32, 8, 128), F32),
            pltpu.VMEM((32, 8, 128), F32),
            pltpu.VMEM((16, 128, 1024), BF16),
            pltpu.VMEM((16, 160, 128), BF16),
            pltpu.VMEM((16, 16, 128), F32),
            pltpu.VMEM((1024, 128), BF16),
            pltpu.VMEM((1024, 1), F32),
            pltpu.VMEM((1024, 1024), F32),
            pltpu.VMEM((8, 1024, 128), F32),
            [pltpu.VMEM((512, 512), BF16), pltpu.VMEM((256, 1024), BF16)],
            [pltpu.VMEM((512, 512), F32), pltpu.VMEM((256, 1024), F32)],
            pltpu.VMEM((4, 128, 1024), F32),
            pltpu.VMEM((3, 128, 1024), WIRE),
            pltpu.VMEM((2, 64, 1024), WIRE),
            pltpu.VMEM((2, 128, 1024), WIRE),
            pltpu.VMEM((8, 8, 128), F32),
            pltpu.VMEM((7, 8, 128), F32),
            dma, dma, dma, dma, dma,
            dma, dma((2, 16)),
            dma, dma((2, 16)),
            dma((4,)), dma((4,)), dma((4,)), dma((2,)), dma((2,)), dma, dma,
        ],
        compiler_params=pltpu.CompilerParams(
            collective_id=0, has_side_effects=True, vmem_limit_bytes=56 << 20),
    )(features, owner_row.reshape(1, 128), owner_row.reshape(128, 1), value_probe, grad_probe)


def solution(mesh):
    placed = (P(("blk", "rep"), None), P(("blk", "rep")), P(None, "blk"), P("blk", None))
    return jax.shard_map(
        per_device,
        mesh=mesh,
        in_specs=placed,
        out_specs=(P(None, ("blk", "rep")), P(("blk", "rep"), None)),
        check_vma=False,
    )
```

time: 383 us -> 70.5 us (0.18)
  waiting for transfers between devices: 119 us -> 0 us
  matrix products: 111 us -> 0 us
  Pallas kernels: 0 us -> 64 us
  local copies, waits for them, and re-layouts: 57.6 us -> 4.55 us
  other arithmetic: 38.1 us -> 0 us
  starting transfers between devices: 31.2 us -> 0 us
  between operations: 14.2 us -> 0.65 us
  blocking collectives: 8.84 us -> 0 us
    dot_general x40 -> x0, matrix products: 111 us -> none  [the longest x8 36.6 us: pair_terms(): jnp.dot(coef_low, col_rows, preferred_element_type=jnp.float32)]
    pallas_call x0 -> x1, Pallas kernels: none -> 64 us  [per_device(): pl.pallas_call(kernel, out_shape=(jax.ShapeDtypeStruct((8, 128), F32), ja...]
    ppermute x27 -> x0, waiting for transfers between devices: 61.3 us -> none  [passed_along(): return lax.ppermute(block, axis, route)]
    reduce_scatter x2 -> x0, waiting for transfers between devices: 48.5 us -> none  [the longest x1 32.1 us: per_device(): lax.psum_scatter(grads, 'rep', scatter_dimension=0, tiled=True)]
    while x70 -> x0, local copies, waits for them, and re-layouts: 30.9 us -> none
    mul x39 -> x0, other arithmetic: 22.5 us -> none  [the longest x8 12.5 us: pair_terms(): (own_wide * scaling)[:, None, :] * sums[:, :, None]]
    all_to_all x2 -> x0, starting transfers between devices: 17.4 us -> none  [the longest x1 10.1 us: per_device(): lax.all_to_all(slots, 'blk', split_axis=0, concat_axis=0, tiled=True)]
    ppermute x27 -> x0, starting transfers between devices: 13.7 us -> none  [passed_along(): return lax.ppermute(block, axis, route)]
  transfers between devices with their start and end apart: 31 -> 0, of which waited for: 14 -> 0; matrix products, arithmetic and copies ran while one was open for 47% -> 0% of each run, Pallas kernels for 0% -> 0%
where the time goes in v1:
time: 70.5 us; the launch traced here: 69.2 us
  Pallas kernels  64 us (91%)
  local copies, waits for them, and re-layouts  4.55 us (6%)
    pallas_call x1, Pallas kernels, per_device(): pl.pallas_call(kernel, out_shape=(jax.ShapeDtypeStruct((8, 128), F32), ja...  64 us
    unnamed x4, local copies, waits for them, and re-layouts  3.81 us

profile of v1, /device:TPU:1, one launch (start us, length us, event | category | flops | bytes accessed | tf_op | source)
XLA Modules:
  0.0 69.2 jit_solution(6888131176037011761)
XLA Ops:
  0.6 0.0 copy-start
  0.6 0.6 copy-done
  1.3 0.7 %copy.6.row_c = s32[128,1]{1,0:T(8,128)} copy(s32[128,1]{0,1:T(1,128)S(1)} %bitcast.3) | data formatting | bytes 1024 | tf_op jit(solution)/shard_map/reshape | solution.py:337
  2.0 64.0 %shard_map.59 = (f32[8,128]{1,0:T(8,128)}, f32[128,1024]{1,0:T(8,128)}) custom-call(bf16[128,128]{1,0:T(8,128)(2,1)} %feat.1, s32[1,128]{1,0:T(1,128)} %bitcast.2, s32[128,1]{1,0:T(8,128)} %copy.6.row_c, bf16[8,512]{1,0:T(8,128)(2,1)} %vprobe.1, bf16[512,1024]{1,0:T(8,128)(2,1)} %gprobe.1), custom_call_target="tpu_custom_call" | custom-call | tf_op jit(solution)/shard_map/pallas_call | solution.py:307
  66.1 1.3 %copy.9 = f32[8,128]{1,0:T(8,128)} copy(f32[8,128]{1,0:T(8,128)} %get-tuple-element.4) | data formatting | bytes 8192
  67.4 1.9 %copy.10 = f32[128,1024]{1,0:T(8,128)} copy(f32[128,1024]{1,0:T(8,128)} %get-tuple-element.5) | data formatting | bytes 1048576
Async XLA Ops:
  0.6 0.7 copy-start
